TPU v7x, 128 devices: a whole 4x4x4 slice. The times are simulated.
128 devices in a mesh: kva: 8 (over y, x_hi), kvb: 16 (over x_lo, z, core).
Axes of the slice: x: 4 (x_hi: 2, x_lo: 2; x = x_hi * 2 + x_lo), y: 4, z: 4, core: 2. Of those that a mesh axis runs over, the one named last changes fastest.
Arguments:
- latent_cache: bfloat16 [2, 786432, 576], P(None, ('kva', 'kvb')), may hold values from -5 to 5
- lengths: int32 [2], replicated, may hold values from 196608 to 786432, as said below
- queries: bfloat16 [2, 2, 128, 576], replicated, may hold values from -24 to 24
- residual_in: bfloat16 [4, 7168], replicated, may hold values from -6 to 6
- value_up: bfloat16 [128, 512, 128], P(('kva', 'kvb')), may hold values from -0.25 to 0.25
- out_weight: bfloat16 [16384, 7168], P(('kva', 'kvb')), may hold values from -0.1875 to 0.1875
- norm_gain: bfloat16 [7168], replicated, may hold values from 0.5 to 1.5
- gate_weight: bfloat16 [7168, 18432], P(None, ('kva', 'kvb')), may hold values from -0.0625 to 0.0625
- up_weight: bfloat16 [7168, 18432], P(None, ('kva', 'kvb')), may hold values from -0.0625 to 0.0625
- down_weight: bfloat16 [18432, 7168], P(('kva', 'kvb')), may hold values from -0.15625 to 0.15625
Outputs:
- head_values: bfloat16 [4, 16384], P(None, ('kva', 'kvb'))
- mixed: bfloat16 [4, 7168], P(None, ('kva', 'kvb'))
Inputs may be any that keep to these rules, and one draw needn't show every extreme that they name: `lengths`: each length is a multiple of 256; in every draw one request's length is exactly 786432.
All inputs are finite; a program needn't handle non-finite values.
Results may differ from a plain program's by a relative error of at most 0.02.
Values may be sent and summed in bfloat16 or wider, within the bound.
A program may use at most 128 MiB of HBM per device.

v0:
```python
import jax
import jax.numpy as jnp
from jax import lax
from jax.sharding import PartitionSpec as P

ROPE = 64
NOPE = 128


def merge_sources(values, peaks, totals):
    summit = jnp.max(peaks, axis=0)
    factor = jnp.exp(peaks - summit[None])
    return (
        jnp.sum(factor[..., None] * values.astype(jnp.float32), axis=0),
        summit,
        jnp.sum(factor * totals, axis=0),
    )


def per_device(
    latent_cache,
    lengths,
    queries,
    residual_in,
    value_up,
    out_weight,
    norm_gain,
    gate_weight,
    up_weight,
    down_weight,
):
    requests = latent_cache.shape[0]
    cache_rows = latent_cache.shape[1]
    query_count = queries.shape[1]
    head_count = queries.shape[2]
    head_own = value_up.shape[0]
    latent = value_up.shape[1]
    value_width = value_up.shape[2]
    token_rows = requests * query_count
    device_id = lax.axis_index(("kva", "kvb"))
    positions = device_id * cache_rows + jnp.arange(cache_rows, dtype=jnp.int32)
    visible = lengths[:, None] - query_count + 1 + jnp.arange(query_count, dtype=jnp.int32)[None, :]
    usable = (positions[None, None, :] < visible[:, :, None])[None]
    scores = jnp.einsum(
        "rjhc,rpc->hrjp", queries, latent_cache, preferred_element_type=jnp.float32
    ) * (NOPE + ROPE) ** (-0.5)
    seg_max = jnp.max(jnp.where(usable, scores, -1e30), axis=-1)
    weights = jnp.where(usable, jnp.exp(scores - seg_max[..., None]), 0.0).astype(jnp.bfloat16)
    seg_total = jnp.sum(weights, axis=-1, dtype=jnp.float32)
    seg_numer = jnp.einsum(
        "hrjp,rpc->hrjc", weights, latent_cache[:, :, :latent], preferred_element_type=jnp.float32
    )
    divisor = jnp.maximum(seg_total, 1.0)
    seg_out = (
        (seg_numer / divisor[..., None])
        .astype(jnp.bfloat16)
        .reshape(head_count, token_rows, latent)
    )
    seg_lse = (seg_max + jnp.log(divisor)).reshape(head_count, token_rows)
    got_out = lax.all_to_all(seg_out, ("kva", "kvb"), split_axis=0, concat_axis=0, tiled=True)
    got_lse = lax.all_to_all(seg_lse, ("kva", "kvb"), split_axis=0, concat_axis=0, tiled=True)
    sources = got_out.shape[0] // head_own
    own_num, own_top, own_tot = merge_sources(
        got_out.reshape(sources, head_own, token_rows, latent),
        got_lse.reshape(sources, head_own, token_rows),
        jnp.ones((sources, head_own, token_rows), jnp.float32),
    )
    attention = (own_num / own_tot[..., None]).astype(jnp.bfloat16)
    head_values = jnp.einsum(
        "grc,gce->rge", attention, value_up, preferred_element_type=jnp.float32
    )
    head_values = head_values.astype(jnp.bfloat16).reshape(token_rows, head_own * value_width)
    projection = jnp.dot(head_values, out_weight, preferred_element_type=jnp.float32)
    width_all = projection.shape[1]
    columns = width_all // lax.axis_size(("kva", "kvb"))
    col_start = device_id * columns
    summed = lax.psum(projection, ("kva", "kvb"))
    attended = (residual_in.astype(jnp.float32) + summed).astype(jnp.bfloat16)
    wide_att = attended.astype(jnp.float32)
    mean_square = jnp.sum(wide_att * wide_att, axis=-1) / width_all
    normed = (
        wide_att * lax.rsqrt(mean_square + 1e-06)[:, None] * norm_gain.astype(jnp.float32)
    ).astype(jnp.bfloat16)
    att_share = lax.dynamic_slice_in_dim(wide_att, col_start, columns, 1)
    gate_part = jnp.dot(normed, gate_weight, preferred_element_type=jnp.float32)
    up_part = jnp.dot(normed, up_weight, preferred_element_type=jnp.float32)
    hidden = (jax.nn.silu(gate_part) * up_part).astype(jnp.bfloat16)
    ffn_part = jnp.dot(hidden, down_weight, preferred_element_type=jnp.float32)
    ffn_share = lax.psum_scatter(ffn_part, ("kva", "kvb"), scatter_dimension=1, tiled=True)
    result_rows = (att_share + ffn_share).astype(jnp.bfloat16)
    return (head_values, result_rows)


def solution(mesh):
    in_specs = (
        P(None, ("kva", "kvb"), None),
        P(),
        P(),
        P(),
        P(("kva", "kvb"), None, None),
        P(("kva", "kvb"), None),
        P(),
        P(None, ("kva", "kvb")),
        P(None, ("kva", "kvb")),
        P(("kva", "kvb"), None),
    )
    out_specs = (P(None, ("kva", "kvb")), P(None, ("kva", "kvb")))
    return jax.shard_map(
        per_device, mesh=mesh, in_specs=in_specs, out_specs=out_specs, check_vma=False
    )
```

profile of v0, /device:TPU:1, one launch (start us, length us, event | category | flops | bytes accessed | tf_op | source)
XLA Modules:
  0.0 369.1 jit_solution(12330908679162895430)
XLA Ops:
  7.2 0.0 copy-start
  7.2 0.8 broadcast_add_fusion
  8.0 0.1 iota_add_fusion.1
  8.1 0.1 broadcast_compare_fusion
  8.2 11.1 %fusion.4 = (f32[128,2,2]{0,2,1:T(2,128)S(1)}, f32[2,6144,2,128]{3,1,2,0:T(8,128)S(1)}) fusion(pred[2,2,6144]{2,1,0:T(4,128)(4,1)S(1)} %broadcast_compare_fusion, bf16[2,2,128,576]{2,3,1,0:T(8,128)(2,1)} %param.12, bf16[2,6144,576]{1,2,0:T(8,128)(2,1)} %param.10), kind=kOutput, calls=%fused_computation.6 | convolution fusion | flops 3633315328 | bytes 27355136 | tf_op jit(solution)/shard_map/rjhc,rpc->hrjp/dot_general | solution.py:44
  19.3 0.0 copy-start.1
  19.3 4.6 %copy-done.1 = f32[2,6144,2,128]{3,1,2,0:T(8,128)} copy-done((f32[2,6144,2,128]{3,1,2,0:T(8,128)}, f32[2,6144,2,128]{3,1,2,0:T(8,128)S(1)}, u32[]{:S(2)}) %copy-start.1) | copy-done | bytes 12582936
  23.9 4.7 %convert_reduce_fusion = f32[128,2,2]{0,2,1:T(2,128)S(1)} fusion(f32[128,2,2]{0,2,1:T(2,128)S(1)} %get-tuple-element.8, f32[2,6144,2,128]{3,1,2,0:T(8,128)S(1)} %get-tuple-element.9, pred[2,2,6144]{2,1,0:T(4,128)(4,1)S(1)} %broadcast_compare_fusion), kind=kLoop, calls=%fused_computation.11 | loop fusion | flops 18873856 | bytes 12611584 | tf_op jit(solution)/shard_map/reduce_sum | solution.py:49
  28.6 0.7 copy.18
  29.3 11.5 %all-to-all-start = ((f32[128,1,4]{2,1,0:T(1,128)}), f32[128,1,4]{2,1,0:T(1,128)S(1)}, u32[]{:S(2)}, u32[]{:S(2)}) async-start(f32[128,1,4]{2,1,0:T(1,128)} %copy.18), calls=%async_computation | async-start | bytes 131072 | tf_op jit(solution)/shard_map/all_to_all | solution.py:61
  40.8 0.0 copy-start.5
  40.8 0.0 copy-start.3
  40.8 0.0 copy-start.2
  40.8 12.5 %fusion.15 = bf16[128,2,2,512]{3,0,2,1:T(8,128)(2,1)S(1)} fusion(bf16[2,6144,576]{1,2,0:T(8,128)(2,1)} %param.10, f32[128,2,2]{0,2,1:T(2,128)S(1)} %get-tuple-element.7, f32[2,6144,2,128]{3,1,2,0:T(8,128)} %copy-done.1, f32[128,2,2]{0,2,1:T(2,128)S(1)} %get-tuple-element.8, pred[2,2,6144]{2,1,0:T(4,128)(4,1)S(1)} %broadcast_compare_fusion), kind=kOutput, calls=%fused_computation.14 | convolution fusion | flops 3234332672 | bytes 25718784 | tf_op jit(solution)/shard_map/hrjp,rpc->hrjc/dot_general | solution.py:50
  53.4 1.2 copy.21
  54.6 0.0 all-to-all-done
  54.6 9.8 %all-to-all-start.1 = ((bf16[128,4,512]{2,1,0:T(4,128)(2,1)}), bf16[128,4,512]{2,1,0:T(4,128)(2,1)S(1)}, u32[]{:S(2)}, u32[]{:S(2)}) async-start(bf16[128,4,512]{2,1,0:T(4,128)(2,1)} %copy.21), calls=%async_computation.1 | async-start | bytes 1048576 | tf_op jit(solution)/shard_map/all_to_all | solution.py:60
  64.4 0.0 all-reduce.4.cloned.1.call-start
  64.4 0.2 reduce_max.19
  64.6 0.2 fusion.36
  64.7 13.2 %all-to-all-done.1 = bf16[128,4,512]{2,1,0:T(4,128)(2,1)S(1)} async-done(((bf16[128,4,512]{2,1,0:T(4,128)(2,1)}), bf16[128,4,512]{2,1,0:T(4,128)(2,1)S(1)}, u32[]{:S(2)}, u32[]{:S(2)}) %all-to-all-start.1) | async-done | bytes 524320 | tf_op jit(solution)/shard_map/all_to_all | solution.py:60
  77.9 0.3 multiply_reduce_fusion
  78.3 0.0 copy-done.5
  78.3 0.2 convolution_convert_fusion
  78.5 0.0 copy-start.4
  78.5 2.5 fusion.37
  81.0 0.0 all-reduce.4.cloned.1.call-update
  81.0 0.0 all-reduce.6.cloned.1.call-start
  81.0 0.0 copy-done.3
  81.1 135.8 %all-reduce.4.cloned.1.call-done = f32[4,7168]{1,0:T(4,128)} async-done(((f32[4,7168]{1,0:T(4,128)}), f32[4,7168]{1,0:T(4,128)}) %all-reduce.4.cloned.1.call-update) | async-done | bytes 114704 | tf_op jit(solution)/shard_map/psum | solution.py:77
  216.8 0.0 copy-done.2
  216.8 1.1 multiply_reduce_fusion.1
  217.9 2.2 fusion.34
  220.2 0.0 copy-done
  220.2 3.8 %fusion.19 = f32[4,7168]{1,0:T(4,128)} fusion(bf16[144,7168]{1,0:T(8,128)(2,1)S(1)} %copy-done, bf16[7168,144]{0,1:T(8,128)(2,1)} %param.18, f32[4,144]{1,0:T(4,128)S(1)} %fusion.34, f32[4,7168]{1,0:T(4,128)S(1)} %get-tuple-element.3, f32[7168]{0:T(1024)S(1)} %convert_element_type.71, f32[4]{0:T(128)S(1)} %add_rsqrt_fusion), kind=kOutput, calls=%fused_computation.17 | convolution fusion | flops 16604544 | bytes 4389136 | tf_op jit(solution)/shard_map/dot_general | solution.py:88
  224.0 0.0 all-reduce.6.cloned.1.call-update
  224.0 136.9 %all-reduce.6.cloned.1.call-done = f32[4,7168]{1,0:T(4,128)} async-done(((f32[4,7168]{1,0:T(4,128)}), f32[4,7168]{1,0:T(4,128)}) %all-reduce.6.cloned.1.call-update) | async-done | bytes 114704
  360.9 1.3 fusion.29
  362.2 0.0 copy-done.4
  (4 shorter events, 0.0 us)
Async XLA Ops:
  7.2 213.0 %copy-start = (bf16[144,7168]{1,0:T(8,128)(2,1)S(1)}, bf16[144,7168]{1,0:T(8,128)(2,1)}, u32[]{:S(2)}) copy-start(bf16[144,7168]{1,0:T(8,128)(2,1)} %param.19) | copy-start | bytes 6193156
  19.3 4.6 %copy-start.1 = (f32[2,6144,2,128]{3,1,2,0:T(8,128)}, f32[2,6144,2,128]{3,1,2,0:T(8,128)S(1)}, u32[]{:S(2)}) copy-start(f32[2,6144,2,128]{3,1,2,0:T(8,128)S(1)} %get-tuple-element.9) | copy-start | bytes 37748740
  29.3 25.3 %all-to-all-start = ((f32[128,1,4]{2,1,0:T(1,128)}), f32[128,1,4]{2,1,0:T(1,128)S(1)}, u32[]{:S(2)}, u32[]{:S(2)}) async-start(f32[128,1,4]{2,1,0:T(1,128)} %copy.18), calls=%async_computation | async-start | bytes 131072 | tf_op jit(solution)/shard_map/all_to_all | solution.py:61
  40.8 37.5 %copy-start.5 = (bf16[1,512,128]{2,1,0:T(8,128)(2,1)S(1)}, bf16[1,512,128]{2,1,0:T(8,128)(2,1)}, u32[]{:S(2)}) copy-start(bf16[1,512,128]{2,1,0:T(8,128)(2,1)} %param.14) | copy-start | bytes 393220
  40.8 40.2 %copy-start.3 = (bf16[7168]{0:T(1024)(128)(2,1)S(1)}, bf16[7168]{0:T(1024)(128)(2,1)}, u32[]{:S(2)}) copy-start(bf16[7168]{0:T(1024)(128)(2,1)} %param.16) | copy-start | bytes 43012
  40.8 176.0 %copy-start.2 = (bf16[4,7168]{1,0:T(4,128)(2,1)S(1)}, bf16[4,7168]{1,0:T(4,128)(2,1)}, u32[]{:S(2)}) copy-start(bf16[4,7168]{1,0:T(4,128)(2,1)} %param.13) | copy-start | bytes 172036
  54.6 23.3 %all-to-all-start.1 = ((bf16[128,4,512]{2,1,0:T(4,128)(2,1)}), bf16[128,4,512]{2,1,0:T(4,128)(2,1)S(1)}, u32[]{:S(2)}, u32[]{:S(2)}) async-start(bf16[128,4,512]{2,1,0:T(4,128)(2,1)} %copy.21), calls=%async_computation.1 | async-start | bytes 1048576 | tf_op jit(solution)/shard_map/all_to_all | solution.py:60
  64.4 152.5 %all-reduce.4.cloned.1.call-start = ((), (), s32[]{:S(2)}) async-start(), calls=%async_computation.2 | async-start | bytes 229376 | tf_op jit(solution)/shard_map/psum | solution.py:77
  78.5 283.8 %copy-start.4 = (bf16[4,128]{1,0:T(4,128)(2,1)}, bf16[4,128]{1,0:T(4,128)(2,1)S(1)}, u32[]{:S(2)}) copy-start(bf16[4,128]{1,0:T(4,128)(2,1)S(1)} %convolution_convert_fusion) | copy-start | bytes 3076
  81.0 279.9 %all-reduce.6.cloned.1.call-start = ((), (), s32[]{:S(2)}) async-start(), calls=%async_computation.3 | async-start | bytes 229376
Sparse Core Ops, SparseCore 0:
  81.1 135.6 all-reduce.3
  224.1 136.7 all-reduce.5
where the time goes:
time: 369 us
  waiting for transfers between devices  286 us (78%)
  matrix products  32.4 us (9%)
  starting transfers between devices  21.3 us (6%)
  between operations  14.2 us (4%)
  other arithmetic  8.73 us (2%)
  local copies, waits for them, and re-layouts  6.52 us (2%)
    unnamed x3, waiting for transfers between devices  137 us
    psum x1, waiting for transfers between devices, per_device(): summed = lax.psum(projection, ('kva', 'kvb'))  136 us
    all_to_all x1, waiting for transfers between devices, per_device(): lax.all_to_all(seg_out, ('kva', 'kvb'), split_axis=0, concat_axis=0, tile...  13.2 us
    dot_general x1, matrix products, per_device(): jnp.einsum('hrjp,rpc->hrjc', weights, latent_cache[:, :, :latent], prefer...  12.5 us
    all_to_all x1, starting transfers between devices, per_device(): lax.all_to_all(seg_lse, ('kva', 'kvb'), split_axis=0, concat_axis=0, tile...  11.5 us
    dot_general x1, matrix products, per_device(): jnp.einsum('rjhc,rpc->hrjp', queries, latent_cache, preferred_element_typ...  11.1 us
    all_to_all x1, starting transfers between devices, per_device(): lax.all_to_all(seg_out, ('kva', 'kvb'), split_axis=0, concat_axis=0, tile...  9.76 us
  transfers between devices with their start and end apart: 4, of which 3 were waited for; matrix products, arithmetic and copies ran while one was open for 4% of the time, Pallas kernels for 0%

commit v1 on v0

v1 whole, which is shorter than its diff:
```python
import functools
import math

import jax
import jax.numpy as jnp
from jax import lax
from jax.experimental import pallas as pl
from jax.experimental.pallas import tpu as pltpu
from jax.sharding import PartitionSpec as P

ROPE = 64
NOPE = 128
SCALE = (NOPE + ROPE) ** (-0.5)
NEG = -1e30
CHUNK = 1024
BF = jnp.bfloat16
F32 = jnp.float32
NT = (((1,), (1,)), ((), ()))
MESH = pl.DeviceIdType.MESH


def split3(x):
    hi = x.astype(BF).astype(F32)
    rest = x - hi
    mid = rest.astype(BF).astype(F32)
    return hi, mid, (rest - mid).astype(BF).astype(F32)


def kernel(
    na,
    nb,
    lengths,
    cache,
    queries,
    residual,
    value_up,
    out_w,
    gain,
    gate_w,
    up_w,
    down_w,
    hv_out,
    mix_out,
    kbuf,
    qbuf,
    sbuf,
    resbuf,
    vbuf,
    owbuf,
    gainbuf,
    gbuf,
    ubuf,
    dbuf,
    msg1,
    rcv1,
    x2,
    msg2,
    rcv2,
    stack,
    msg3,
    rcv3,
    msg4,
    rcv4,
    msg5,
    rcv5,
    wide,
    msg6,
    rcv6,
    msg7,
    rcv7,
    ksem,
    wsem,
    ssem,
    rsem,
):
    a = lax.axis_index("kva")
    b = lax.axis_index("kvb")
    requests, width, rows = kbuf.shape
    nq, heads = qbuf.shape[1], qbuf.shape[3]
    latent = vbuf.shape[1]
    qrows = nq * heads
    tokens = requests * nq
    d_model = owbuf.shape[1]
    block = d_model // na
    tiles = block // 128
    group = heads // na
    pieces = latent // 128
    chunks = rows // CHUNK
    ext = latent + 128

    def peer_a(k):
        return lax.rem(a + k, na)

    def peer_b(k):
        return lax.rem(b + k, nb)

    qcopy = pltpu.make_async_copy(queries, qbuf, wsem.at[0])
    qcopy.start()
    kcopies = []
    for r in range(requests):
        for c in range(chunks):
            part = pl.ds(c * CHUNK, CHUNK)
            copy = pltpu.make_async_copy(
                cache.at[r, :, part], kbuf.at[r, :, part], ksem.at[r * chunks + c]
            )
            copy.start()
            kcopies.append(copy)
    barrier = pltpu.get_barrier_semaphore()
    for k in range(1, na):
        pl.semaphore_signal(barrier, inc=1, device_id=(peer_a(k), b), device_id_type=MESH)
    for k in range(1, nb):
        pl.semaphore_signal(barrier, inc=1, device_id=(a, peer_b(k)), device_id_type=MESH)
    weights = [
        pltpu.make_async_copy(src, dst, wsem.at[i + 1])
        for i, (src, dst) in enumerate(
            (
                (value_up, vbuf),
                (out_w, owbuf),
                (residual, resbuf),
                (gain, gainbuf),
                (gate_w, gbuf),
                (up_w, ubuf),
                (down_w, dbuf),
            )
        )
    ]

    def send(stage, src, dst, device):
        pltpu.make_async_remote_copy(
            src_ref=src,
            dst_ref=dst,
            send_sem=ssem.at[stage],
            recv_sem=rsem.at[stage],
            device_id=device,
            device_id_type=MESH,
        ).start()

    def arrived(stage, buf):
        pltpu.make_async_copy(buf, buf, rsem.at[stage]).wait()

    def sent(stage, buf):
        pltpu.make_async_copy(buf, buf, ssem.at[stage]).wait()

    first = (a * nb + b) * rows
    factor = SCALE * math.log2(math.e)
    qcopy.wait()
    for r in range(requests):
        q = jnp.concatenate([qbuf[r, j].T for j in range(nq)], axis=0)
        peak = None
        for c in range(chunks):
            part = pl.ds(c * CHUNK, CHUNK)
            kcopies[r * chunks + c].wait()
            s = jnp.dot(q, kbuf[r, :, part], preferred_element_type=F32)
            pos = first + c * CHUNK + lax.broadcasted_iota(jnp.int32, (1, CHUNK), 1)
            halves = []
            for j in range(nq):
                bias = jnp.where(pos < lengths[r] - (nq - 1) + j, 0.0, NEG)
                halves.append(s[j * heads : (j + 1) * heads] + bias)
            s = jnp.concatenate(halves, axis=0)
            sbuf[:, part] = s
            for t in range(CHUNK // 128):
                tile = s[:, t * 128 : (t + 1) * 128]
                peak = tile if peak is None else jnp.maximum(peak, tile)
        if r == 0:
            for copy in weights:
                copy.start()
        top = jnp.max(peak, axis=1, keepdims=True)
        shift = top * factor
        total = jnp.zeros((qrows, 128), F32)
        numer = jnp.zeros((qrows, latent), F32)
        for c in range(chunks):
            part = pl.ds(c * CHUNK, CHUNK)
            w = jnp.exp2(sbuf[:, part] * factor - shift)
            for t in range(CHUNK // 128):
                total = total + w[:, t * 128 : (t + 1) * 128]
            numer = numer + lax.dot_general(
                w.astype(BF), kbuf[r, :latent, part], NT, preferred_element_type=F32
            )
        total = jnp.sum(total, axis=1, keepdims=True)
        lse = top * SCALE + jnp.log(total)
        out = (numer * (1.0 / total)).astype(BF)
        lane = lax.broadcasted_iota(jnp.int32, (1, 128), 1)
        hi, mid, lo = split3(lse)
        tail = jnp.where(lane == 0, hi, jnp.where(lane == 1, mid, jnp.where(lane == 2, lo, 0.0)))
        msg1[r, :, :, :latent] = out.reshape(nq, heads, latent)
        msg1[r, :, :, latent:] = tail.astype(BF).reshape(nq, heads, 128)
        if r == 0:
            pl.semaphore_wait(barrier, na + nb - 2)
        for k in range(1, na):
            p = peer_a(k)
            send(
                r,
                msg1.at[r, :, pl.ds(pl.multiple_of(p * group, group), group), :],
                rcv1.at[r, k - 1],
                (p, b),
            )

    for r in range(requests):
        arrived(r, rcv1.at[r])
        mine = msg1[r, :, pl.ds(pl.multiple_of(a * group, group), group), :]
        parts = [mine] + [rcv1[r, k] for k in range(na - 1)]
        for j in range(nq):
            vals = [x[j, :, :latent].astype(F32) for x in parts]
            tails = [x[j, :, latent:].astype(F32) for x in parts]
            lses = [jnp.sum(t, axis=1, keepdims=True) for t in tails]
            top = functools.reduce(jnp.maximum, lses)
            ws = [jnp.exp(x - top) for x in lses]
            den = functools.reduce(jnp.add, ws)
            num = functools.reduce(jnp.add, [w * v for w, v in zip(ws, vals)])
            val = num * (1.0 / den)
            lse = top + jnp.log(den)
            rj = r * nq + j
            for c in range(pieces):
                x2[:, c * tokens + rj, :] = val[:, c * 128 : (c + 1) * 128]
            for c, piece in enumerate(split3(jnp.broadcast_to(lse, (group, 128)))):
                x2[:, (pieces + c) * tokens + rj, :] = piece
    for c in range((pieces + 3) * tokens, x2.shape[1]):
        x2[:, c, :] = jnp.zeros((group, 128), F32)
    msg2[...] = x2[...].astype(BF)
    for k in range(1, nb):
        p = peer_b(k)
        send(2, msg2.at[p], rcv2.at[k - 1], (a, p))

    arrived(2, rcv2)
    parts = [msg2[b].astype(F32)] + [rcv2[k].astype(F32) for k in range(nb - 1)]
    edge = pieces * tokens
    lses = [
        x[edge : edge + tokens] + x[edge + tokens : edge + 2 * tokens] + x[edge + 2 * tokens : edge + 3 * tokens]
        for x in parts
    ]
    top = functools.reduce(jnp.maximum, lses)
    ws = [jnp.exp(x - top) for x in lses]
    den = 1.0 / functools.reduce(jnp.add, ws)
    for copy in weights[:1]:
        copy.wait()
    head_values = jnp.zeros((tokens, 128), F32)
    for c in range(pieces):
        num = functools.reduce(
            jnp.add, [w * x[c * tokens : (c + 1) * tokens] for w, x in zip(ws, parts)]
        )
        head_values = head_values + jnp.dot(
            (num * den).astype(BF), vbuf[0, c * 128 : (c + 1) * 128, :], preferred_element_type=F32
        )
    head_values = head_values.astype(BF)
    hv_out[...] = head_values

    def scatter(stage, lhs, wbuf, msg, rcv):
        for k in range(1, na + 1):
            p = peer_a(k)
            y = jnp.dot(
                lhs,
                wbuf[:, pl.ds(pl.multiple_of(p * block, 128), block)],
                preferred_element_type=F32,
            )
            for t in range(tiles):
                stack[k - 1, t * tokens : (t + 1) * tokens, :] = y[:, t * 128 : (t + 1) * 128]
            if k < na:
                msg[k - 1] = stack[k - 1].astype(BF)
                send(stage, msg.at[k - 1], rcv.at[k - 1], (p, b))
        arrived(stage, rcv)
        return functools.reduce(
            jnp.add, [stack[na - 1]] + [rcv[k].astype(F32) for k in range(na - 1)]
        )

    def spread(stage, x, msg, rcv):
        msg[...] = x.astype(BF)
        for k in range(1, nb):
            send(stage, msg, rcv.at[k - 1], (a, peer_b(k)))
        arrived(stage, rcv)
        return functools.reduce(jnp.add, [x] + [rcv[k].astype(F32) for k in range(nb - 1)])

    for copy in weights[1:]:
        copy.wait()
    stack[...] = jnp.zeros(stack.shape, F32)
    summed = spread(4, scatter(3, head_values, owbuf, msg3, rcv3), msg4, rcv4)
    for t in range(tiles):
        stack[0, t * tokens : (t + 1) * tokens, :] = resbuf[
            :, pl.ds(pl.multiple_of(a * block + t * 128, 128), 128)
        ].astype(F32)
    attended = (stack[0] + summed).astype(BF)
    msg5[...] = attended
    for k in range(1, na):
        send(5, msg5, rcv5.at[k - 1], (peer_a(k), b))
    attended = attended.astype(F32)
    arrived(5, rcv5)
    for k in range(na):
        p = lax.rem(a - k + na, na)
        x = attended if k == 0 else rcv5[k - 1].astype(F32)
        for t in range(tiles):
            wide[:, pl.ds(pl.multiple_of(p * block + t * 128, 128), 128)] = x[
                t * tokens : (t + 1) * tokens
            ]
    att = wide[...]
    mean_square = jnp.sum(att * att, axis=1, keepdims=True) / d_model
    normed = (
        att * lax.rsqrt(mean_square + 1e-06) * gainbuf[...].astype(F32).reshape(1, d_model)
    ).astype(BF)
    gate = lax.dot_general(normed, gbuf[...], NT, preferred_element_type=F32)
    up = lax.dot_general(normed, ubuf[...], NT, preferred_element_type=F32)
    hidden = (gate / (1.0 + jnp.exp(-gate)) * up).astype(BF)
    ffn = spread(7, scatter(6, hidden, dbuf, msg6, rcv6), msg7, rcv7)
    mixed = (attended + ffn).astype(BF).astype(F32)

    own = mix_out.shape[1]
    picked = jnp.zeros((tokens, own), F32)
    for t in range(tiles):
        row = t * 128 + lax.broadcasted_iota(jnp.int32, (128, own), 0)
        col = b * own + lax.broadcasted_iota(jnp.int32, (128, own), 1)
        pick = jnp.where(row == col, 1.0, 0.0).astype(BF)
        picked = picked + jnp.dot(
            mixed[t * tokens : (t + 1) * tokens].astype(BF), pick, preferred_element_type=F32
        )
    mix_out[...] = picked.astype(BF)

    for r in range(requests):
        sent(r, rcv1.at[r])
    for stage, buf in ((2, rcv2), (3, rcv3), (4, rcv4), (5, rcv5), (6, rcv6), (7, rcv7)):
        sent(stage, buf)


def per_device(
    na,
    nb,
    latent_cache,
    lengths,
    queries,
    residual_in,
    value_up,
    out_weight,
    norm_gain,
    gate_weight,
    up_weight,
    down_weight,
):
    latent_cache = jnp.swapaxes(latent_cache, 1, 2)
    queries = jnp.swapaxes(queries, 2, 3)
    gate_weight = gate_weight.T
    up_weight = up_weight.T
    rows = latent_cache.shape[2]
    requests, nq, _, heads = queries.shape
    latent = value_up.shape[1]
    tokens, d_model = residual_in.shape
    group = heads // na
    ext = latent + 128
    lines = 32
    chunks = rows // CHUNK
    vmem = pltpu.VMEM
    scratch = [
        vmem(latent_cache.shape, BF),
        vmem(queries.shape, BF),
        vmem((nq * heads, rows), F32),
        vmem(residual_in.shape, BF),
        vmem(value_up.shape, BF),
        vmem(out_weight.shape, BF),
        vmem(norm_gain.shape, BF),
        vmem(gate_weight.shape, BF),
        vmem(up_weight.shape, BF),
        vmem(down_weight.shape, BF),
        vmem((requests, nq, heads, ext), BF),
        vmem((requests, na - 1, nq, group, ext), BF),
        vmem((group, lines, 128), F32),
        vmem((group, lines, 128), BF),
        vmem((nb - 1, lines, 128), BF),
        vmem((na, lines, 128), F32),
        vmem((na - 1, lines, 128), BF),
        vmem((na - 1, lines, 128), BF),
        vmem((lines, 128), BF),
        vmem((nb - 1, lines, 128), BF),
        vmem((lines, 128), BF),
        vmem((na - 1, lines, 128), BF),
        vmem((tokens, d_model), F32),
        vmem((na - 1, lines, 128), BF),
        vmem((na - 1, lines, 128), BF),
        vmem((lines, 128), BF),
        vmem((nb - 1, lines, 128), BF),
        pltpu.SemaphoreType.DMA((requests * chunks,)),
        pltpu.SemaphoreType.DMA((8,)),
        pltpu.SemaphoreType.DMA((8,)),
        pltpu.SemaphoreType.DMA((8,)),
    ]
    anywhere = pl.BlockSpec(memory_space=pl.ANY)
    return pl.pallas_call(
        functools.partial(kernel, na, nb),
        out_shape=(
            jax.ShapeDtypeStruct((tokens, value_up.shape[0] * value_up.shape[2]), BF),
            jax.ShapeDtypeStruct((tokens, d_model // (na * nb)), BF),
        ),
        in_specs=[pl.BlockSpec(memory_space=pltpu.SMEM)] + [anywhere] * 9,
        out_specs=(pl.BlockSpec(memory_space=pltpu.VMEM), pl.BlockSpec(memory_space=pltpu.VMEM)),
        scratch_shapes=scratch,
        compiler_params=pltpu.CompilerParams(
            collective_id=0, has_side_effects=True, vmem_limit_bytes=60 * 1024 * 1024
        ),
    )(
        lengths,
        latent_cache,
        queries,
        residual_in,
        value_up,
        out_weight,
        norm_gain,
        gate_weight,
        up_weight,
        down_weight,
    )


def solution(mesh):
    na, nb = mesh.shape["kva"], mesh.shape["kvb"]
    both = ("kva", "kvb")
    in_specs = (
        P(None, both, None),
        P(),
        P(),
        P(),
        P(both, None, None),
        P(both, None),
        P(),
        P(None, both),
        P(None, both),
        P(both, None),
    )
    out_specs = (P(None, both), P(None, both))
    return jax.shard_map(
        functools.partial(per_device, na, nb),
        mesh=mesh,
        in_specs=in_specs,
        out_specs=out_specs,
        check_vma=False,
    )
```

time: 369 us -> 64.6 us (0.18)
  waiting for transfers between devices: 286 us -> 0 us
  Pallas kernels: 0 us -> 61.3 us
  matrix products: 32.4 us -> 0 us
  starting transfers between devices: 21.3 us -> 0 us
  between operations: 14.2 us -> 0.64 us
  other arithmetic: 8.73 us -> 0 us
  local copies, waits for them, and re-layouts: 6.52 us -> 2.44 us
    unnamed x3 -> x0, waiting for transfers between devices: 137 us -> none
    psum x1 -> x0, waiting for transfers between devices: 136 us -> none  [per_device(): summed = lax.psum(projection, ('kva', 'kvb'))]
    pallas_call x0 -> x1, Pallas kernels: none -> 61.3 us  [per_device(): pl.pallas_call(functools.partial(kernel, na, nb), out_shape=(jax.ShapeDty...]
    dot_general x6 -> x0, matrix products: 32.4 us -> none  [the longest x1 12.5 us: per_device(): jnp.einsum('hrjp,rpc->hrjc', weights, latent_cache[:, :, :latent], prefer...]
    all_to_all x2 -> x0, starting transfers between devices: 21.3 us -> none  [the longest x1 11.5 us: per_device(): lax.all_to_all(seg_lse, ('kva', 'kvb'), split_axis=0, concat_axis=0, tile...]
    all_to_all x2 -> x0, waiting for transfers between devices: 13.2 us -> none  [the longest x1 13.2 us: per_device(): lax.all_to_all(seg_out, ('kva', 'kvb'), split_axis=0, concat_axis=0, tile...]
    reduce_sum x4 -> x0, other arithmetic: 6.23 us -> none  [the longest x1 4.66 us: per_device(): seg_total = jnp.sum(weights, axis=-1, dtype=jnp.float32)]
  transfers between devices with their start and end apart: 4 -> 0, of which waited for: 3 -> 0; matrix products, arithmetic and copies ran while one was open for 4% -> 0% of each run, Pallas kernels for 0% -> 0%
where the time goes in v1:
time: 64.6 us; the launch traced here: 64.4 us
  Pallas kernels  61.3 us (95%)
  local copies, waits for them, and re-layouts  2.44 us (4%)
    pallas_call x1, Pallas kernels, per_device(): pl.pallas_call(functools.partial(kernel, na, nb), out_shape=(jax.ShapeDty...  61.3 us
    unnamed x2, local copies, waits for them, and re-layouts  2.44 us

profile of v1, /device:TPU:1, one launch (start us, length us, event | category | flops | bytes accessed | tf_op | source)
XLA Modules:
  0.0 64.4 jit_solution(5010226276894194680)
XLA Ops:
  0.6 61.3 %shard_map.113 = (bf16[4,128]{1,0:T(4,128)(2,1)}, bf16[4,56]{1,0:T(4,128)(2,1)}) custom-call(s32[2]{0:T(128)} %lengths.1, bf16[2,576,6144]{2,1,0:T(8,128)(2,1)} %bitcast.4, bf16[2,2,576,128]{3,2,1,0:T(8,128)(2,1)} %bitcast.7, bf16[4,7168]{1,0:T(4,128)(2,1)} %residual.1, bf16[1,512,128]{2,1,0:T(8,128)(2,1)} %value_up.1, bf16[128,7168]{1,0:T(8,128)(2,1)} %out_w.1, ...), custom_call_target="tpu_custom_call" | custom-call | tf_op jit(solution)/shard_map/pallas_call | solution.py:382
  62.0 1.2 %copy.14 = bf16[4,128]{1,0:T(4,128)(2,1)} copy(bf16[4,128]{1,0:T(4,128)(2,1)} %get-tuple-element.4) | data formatting | bytes 2048
  63.2 1.2 %copy.15 = bf16[4,56]{1,0:T(4,128)(2,1)} copy(bf16[4,56]{1,0:T(4,128)(2,1)} %get-tuple-element.5) | data formatting | bytes 896

commit v2 on v1

v2 whole, which is shorter than its diff:
```python
import math

import jax
import jax.numpy as jnp
from jax import lax
from jax.experimental import pallas as pl
from jax.experimental.pallas import tpu as pltpu
from jax.sharding import PartitionSpec as P

ROPE = 64
NOPE = 128
SCALE = (NOPE + ROPE) ** (-0.5)
NEG = -1e30
CHUNK = 1024
BF = jnp.bfloat16
F32 = jnp.float32
NT = (((1,), (1,)), ((), ()))
MESH = pl.DeviceIdType.MESH


def split3(x):
    hi = x.astype(BF).astype(F32)
    rest = x - hi
    mid = rest.astype(BF).astype(F32)
    return hi, mid, (rest - mid).astype(BF).astype(F32)


def farthest_first():
    hops = lambda o: sum(min(v, 4 - v) for v in o)
    offsets = [(y, x, z) for y in range(4) for x in range(4) for z in range(4)]
    return sorted(offsets, key=hops, reverse=True)[:-1]


def kernel(
    lengths,
    cache,
    queries,
    residual,
    value_up,
    out_w,
    gain,
    gate_w,
    up_w,
    down_w,
    hv_out,
    mix_out,
    kbuf,
    qbuf,
    sbuf,
    resbuf,
    vbuf,
    owbuf,
    gainbuf,
    gbuf,
    ubuf,
    dbuf,
    msg1,
    rcv1,
    x2,
    msg2,
    rcv2,
    stack,
    resid,
    msg3,
    rcv3,
    msg4,
    rcv4,
    wide,
    msg5,
    rcv5,
    msg6,
    rcv6,
    ksem,
    wsem,
    ssem,
    rsem,
):
    a = lax.axis_index("kva")
    b = lax.axis_index("kvb")
    requests, width, rows = kbuf.shape
    nq, heads = qbuf.shape[1], qbuf.shape[3]
    latent = vbuf.shape[1]
    qrows = nq * heads
    tokens = requests * nq
    d_model = owbuf.shape[1]
    tiles = d_model // 128
    chips = heads // 2
    pieces = latent // 128
    chunks = rows // CHUNK
    own = mix_out.shape[1]

    core = b % 2
    ys = [(a // 2 + k) % 4 for k in range(4)]
    xs = [((a % 2) * 2 + b // 8 + k) % 4 for k in range(4)]
    zs = [((b // 2) % 4 + k) % 4 for k in range(4)]
    chip = ys[0] * 16 + xs[0] * 4 + zs[0]
    y_part = [y * 2 for y in ys]
    x_part = [x // 2 for x in xs]
    x_low = [(x % 2) * 8 + core for x in xs]
    z_part = [z * 2 for z in zs]
    sibling = (a, b + 1 - 2 * core)

    def device_at(dy, dx, dz):
        return (y_part[dy] + x_part[dx], x_low[dx] + z_part[dz])

    def chip_at(dy, dx, dz):
        return ys[dy] * 16 + xs[dx] * 4 + zs[dz]

    offsets = farthest_first()

    qcopy = pltpu.make_async_copy(queries, qbuf, wsem.at[0])
    qcopy.start()
    kcopies = []
    for r in range(requests):
        for c in range(chunks):
            part = pl.ds(c * CHUNK, CHUNK)
            copy = pltpu.make_async_copy(
                cache.at[r, :, part], kbuf.at[r, :, part], ksem.at[r * chunks + c]
            )
            copy.start()
            kcopies.append(copy)
    weights = [
        pltpu.make_async_copy(src, dst, wsem.at[i + 1])
        for i, (src, dst) in enumerate(
            (
                (value_up, vbuf),
                (residual, resbuf),
                (out_w, owbuf),
                (gain, gainbuf),
                (gate_w, gbuf),
                (up_w, ubuf),
                (down_w, dbuf),
            )
        )
    ]
    barrier = pltpu.get_barrier_semaphore()
    pl.semaphore_signal(barrier, inc=1, device_id=sibling, device_id_type=MESH)
    for off in offsets:
        pl.semaphore_signal(barrier, inc=1, device_id=device_at(*off), device_id_type=MESH)

    def send(stage, src, dst, device):
        pltpu.make_async_remote_copy(
            src_ref=src,
            dst_ref=dst,
            send_sem=ssem.at[stage],
            recv_sem=rsem.at[stage],
            device_id=device,
            device_id_type=MESH,
        ).start()

    def arrived(stage, buf):
        pltpu.make_async_copy(buf, buf, rsem.at[stage]).wait()

    def sent(stage, buf):
        pltpu.make_async_copy(buf, buf, ssem.at[stage]).wait()

    first = (a * 16 + b) * rows
    factor = SCALE * math.log2(math.e)

    def scores(r):
        at = lax.broadcasted_iota(jnp.int32, (heads, heads), 0)
        head = lax.broadcasted_iota(jnp.int32, (heads, heads), 1)
        order = jnp.where(head == (at % chips) * 2 + at // chips, 1.0, 0.0).astype(BF)
        q = jnp.concatenate(
            [
                lax.dot_general(order, qbuf[r, j], NT, preferred_element_type=F32).astype(BF)
                for j in range(nq)
            ],
            axis=0,
        )
        peak = None
        for c in range(chunks):
            part = pl.ds(c * CHUNK, CHUNK)
            kcopies[r * chunks + c].wait()
            s = jnp.dot(q, kbuf[r, :, part], preferred_element_type=F32)
            pos = first + c * CHUNK + lax.broadcasted_iota(jnp.int32, (1, CHUNK), 1)
            halves = []
            for j in range(nq):
                bias = jnp.where(pos < lengths[r] - (nq - 1) + j, 0.0, NEG)
                halves.append(s[j * heads : (j + 1) * heads] + bias)
            s = jnp.concatenate(halves, axis=0)
            sbuf[:, part] = s
            for t in range(CHUNK // 128):
                tile = s[:, t * 128 : (t + 1) * 128]
                peak = tile if peak is None else jnp.maximum(peak, tile)
        return jnp.max(peak, axis=1, keepdims=True)

    def values(r, top):
        shift = top * factor
        total = jnp.zeros((qrows, 128), F32)
        numer = jnp.zeros((qrows, latent), F32)
        for c in range(chunks):
            part = pl.ds(c * CHUNK, CHUNK)
            w = jnp.exp2(sbuf[:, part] * factor - shift)
            for t in range(CHUNK // 128):
                total = total + w[:, t * 128 : (t + 1) * 128]
            numer = numer + lax.dot_general(
                w.astype(BF), kbuf[r, :latent, part], NT, preferred_element_type=F32
            )
        total = jnp.sum(total, axis=1, keepdims=True)
        lse = top * SCALE + jnp.log(total)
        out = (numer * (1.0 / total)).astype(BF)
        lane = lax.broadcasted_iota(jnp.int32, (1, 128), 1)
        hi, mid, lo = split3(lse)
        tail = jnp.where(lane == 0, hi, jnp.where(lane == 1, mid, jnp.where(lane == 2, lo, 0.0)))
        tail = tail.astype(BF)
        for half in range(2):
            for j in range(nq):
                at = slice(j * heads + half * chips, j * heads + (half + 1) * chips)
                msg1[r, half, j, :, :latent] = out[at]
                msg1[r, half, j, :, latent:] = tail[at]
        if r == 0:
            pl.semaphore_wait(barrier, len(offsets) + 1)
        send(r, msg1.at[r, 1 - core], rcv1.at[r], sibling)

    def exchange(r):
        arrived(r, rcv1.at[r])
        for j in range(nq):
            parts = [msg1[r, core, j], rcv1[r, j]]
            vals = [x[:, :latent].astype(F32) for x in parts]
            lses = [jnp.sum(x[:, latent:].astype(F32), axis=1, keepdims=True) for x in parts]
            top = jnp.maximum(*lses)
            ws = [jnp.exp(x - top) for x in lses]
            den = ws[0] + ws[1]
            val = (ws[0] * vals[0] + ws[1] * vals[1]) * (1.0 / den)
            lse = top + jnp.log(den)
            for c in range(pieces):
                x2[:, c * nq + j, :] = val[:, c * 128 : (c + 1) * 128]
            for c, piece in enumerate(split3(jnp.broadcast_to(lse, (chips, 128)))):
                x2[:, (pieces + c) * nq + j, :] = piece
        msg2[r] = x2[...].astype(BF)
        for k, off in enumerate(offsets):
            send(2 + r, msg2.at[r, chip_at(*off)], rcv2.at[r, k], device_at(*off))

    def head_rows(r):
        arrived(2 + r, rcv2.at[r, pl.ds(0, len(offsets))])
        rcv2[r, len(offsets)] = msg2[r, chip]
        x = rcv2[r].astype(F32)
        edge = pieces * nq
        lse = (
            x[:, edge : edge + nq]
            + x[:, edge + nq : edge + 2 * nq]
            + x[:, edge + 2 * nq : edge + 3 * nq]
        )
        top = jnp.max(lse, axis=0, keepdims=True)
        w = jnp.exp(lse - top)
        w = w * (1.0 / jnp.sum(w, axis=0, keepdims=True))
        w = jnp.concatenate([w] * pieces, axis=1)
        att = jnp.sum(w * x[:, :edge], axis=0)
        total = jnp.zeros((nq, 128), F32)
        for c in range(pieces):
            total = total + jnp.dot(
                att[c * nq : (c + 1) * nq].astype(BF),
                vbuf[0, c * 128 : (c + 1) * 128, :],
                preferred_element_type=F32,
            )
        return total

    for c in range((pieces + 3) * nq, x2.shape[1]):
        x2[:, c, :] = jnp.zeros((chips, 128), F32)
    qcopy.wait()
    top = scores(0)
    for copy in weights:
        copy.start()
    values(0, top)
    top = scores(1)
    exchange(0)
    values(1, top)
    exchange(1)
    for copy in weights:
        copy.wait()
    for t in range(tiles):
        resid[t * tokens : (t + 1) * tokens, :] = resbuf[:, t * 128 : (t + 1) * 128].astype(F32)
    head_values = jnp.concatenate([head_rows(0), head_rows(1)], axis=0).astype(BF)
    hv_out[...] = head_values

    y = jnp.dot(head_values, owbuf[...], preferred_element_type=F32)
    for t in range(tiles):
        stack[t * tokens : (t + 1) * tokens, :] = y[:, t * 128 : (t + 1) * 128]
    msg3[...] = stack[...].astype(BF)
    send(4, msg3, rcv3, sibling)
    arrived(4, rcv3)
    summed = stack[...] + rcv3[...].astype(F32)
    lines = tiles * tokens
    third = (lines // 3 + 15) // 16 * 16
    for step in range(3):
        msg4[step] = summed.astype(BF)
        for k in (2, 1, 3):
            for g in range(3):
                part = pl.ds(g * third, min(third, lines - g * third))
                off = [0, 0, 0]
                off[(g + step) % 3] = k
                send(
                    5 + step,
                    msg4.at[step, part, :],
                    rcv4.at[step, k - 1, part, :],
                    device_at(*off),
                )
        arrived(5 + step, rcv4.at[step])
        for k in range(3):
            summed = summed + rcv4[step, k].astype(F32)
    stack[...] = (resid[...] + summed).astype(BF).astype(F32)
    for t in range(tiles):
        wide[:, t * 128 : (t + 1) * 128] = stack[t * tokens : (t + 1) * tokens, :]
    att = wide[...]
    mean_square = jnp.sum(att * att, axis=1, keepdims=True) / d_model
    normed = (
        att * lax.rsqrt(mean_square + 1e-06) * gainbuf[...].astype(F32).reshape(1, d_model)
    ).astype(BF)
    gate = lax.dot_general(normed, gbuf[...], NT, preferred_element_type=F32)
    up = lax.dot_general(normed, ubuf[...], NT, preferred_element_type=F32)
    hidden = (gate / (1.0 + jnp.exp(-gate)) * up).astype(BF)

    y = jnp.dot(hidden, dbuf[...], preferred_element_type=F32)
    y = y + jnp.where(chip * 2 + core == 0, att, 0.0)
    y = jnp.concatenate([y, jnp.zeros((tokens, 128), F32)], axis=1)
    for o in range(2 * chips):
        msg5[o % 2, o // 2] = y[:, o * own : o * own + 128]
    send(8, msg5.at[1 - core], rcv5, sibling)
    arrived(8, rcv5)
    msg6[...] = msg5[core] + rcv5[...]
    for k, off in enumerate(offsets):
        send(9, msg6.at[chip_at(*off)], rcv6.at[k], device_at(*off))
    arrived(9, rcv6)
    total = msg6[chip] + jnp.sum(rcv6[...], axis=0)
    mix_out[...] = total[:, :own].astype(BF)

    for r in range(requests):
        sent(r, rcv1.at[r])
        sent(2 + r, rcv2.at[r, pl.ds(0, len(offsets))])
    sent(4, rcv3)
    for step in range(3):
        sent(5 + step, rcv4.at[step])
    sent(8, rcv5)
    sent(9, rcv6)


def per_device(
    latent_cache,
    lengths,
    queries,
    residual_in,
    value_up,
    out_weight,
    norm_gain,
    gate_weight,
    up_weight,
    down_weight,
):
    latent_cache = jnp.swapaxes(latent_cache, 1, 2)
    queries = jnp.swapaxes(queries, 2, 3)
    gate_weight = gate_weight.T
    up_weight = up_weight.T
    rows = latent_cache.shape[2]
    requests, nq, _, heads = queries.shape
    latent = value_up.shape[1]
    tokens, d_model = residual_in.shape
    chips = heads // 2
    lines = tokens * d_model // 128
    vmem = pltpu.VMEM
    scratch = [
        vmem(latent_cache.shape, BF),
        vmem(queries.shape, BF),
        vmem((nq * heads, rows), F32),
        vmem(residual_in.shape, BF),
        vmem(value_up.shape, BF),
        vmem(out_weight.shape, BF),
        vmem(norm_gain.shape, BF),
        vmem(gate_weight.shape, BF),
        vmem(up_weight.shape, BF),
        vmem(down_weight.shape, BF),
        vmem((requests, 2, nq, chips, latent + 128), BF),
        vmem((requests, nq, chips, latent + 128), BF),
        vmem((chips, 16, 128), F32),
        vmem((requests, chips, 16, 128), BF),
        vmem((requests, chips, 16, 128), BF),
        vmem((lines, 128), F32),
        vmem((lines, 128), F32),
        vmem((lines, 128), BF),
        vmem((lines, 128), BF),
        vmem((3, lines, 128), BF),
        vmem((3, 3, lines, 128), BF),
        vmem((tokens, d_model), F32),
        vmem((2, chips, tokens, 128), F32),
        vmem((chips, tokens, 128), F32),
        vmem((chips, tokens, 128), F32),
        vmem((chips - 1, tokens, 128), F32),
        pltpu.SemaphoreType.DMA((requests * (rows // CHUNK),)),
        pltpu.SemaphoreType.DMA((8,)),
        pltpu.SemaphoreType.DMA((10,)),
        pltpu.SemaphoreType.DMA((10,)),
    ]
    anywhere = pl.BlockSpec(memory_space=pl.ANY)
    return pl.pallas_call(
        kernel,
        out_shape=(
            jax.ShapeDtypeStruct((tokens, value_up.shape[0] * value_up.shape[2]), BF),
            jax.ShapeDtypeStruct((tokens, d_model // heads), BF),
        ),
        in_specs=[pl.BlockSpec(memory_space=pltpu.SMEM)] + [anywhere] * 9,
        out_specs=(pl.BlockSpec(memory_space=pltpu.VMEM), pl.BlockSpec(memory_space=pltpu.VMEM)),
        scratch_shapes=scratch,
        compiler_params=pltpu.CompilerParams(
            collective_id=0, has_side_effects=True, vmem_limit_bytes=60 * 1024 * 1024
        ),
    )(
        lengths,
        latent_cache,
        queries,
        residual_in,
        value_up,
        out_weight,
        norm_gain,
        gate_weight,
        up_weight,
        down_weight,
    )


def solution(mesh):
    both = ("kva", "kvb")
    in_specs = (
        P(None, both, None),
        P(),
        P(),
        P(),
        P(both, None, None),
        P(both, None),
        P(),
        P(None, both),
        P(None, both),
        P(both, None),
    )
    out_specs = (P(None, both), P(None, both))
    return jax.shard_map(
        per_device,
        mesh=mesh,
        in_specs=in_specs,
        out_specs=out_specs,
        check_vma=False,
    )
```

time: 64.6 us -> 57.5 us (0.89)
  Pallas kernels: 61.3 us -> 54.3 us
    pallas_call x1, Pallas kernels: 61.3 us -> 54.3 us  [per_device(): pl.pallas_call(kernel, out_shape=(jax.ShapeDtypeStruct((tokens, value_up....]
where the time goes in v2:
time: 57.5 us; the launch traced here: 57.4 us
  Pallas kernels  54.3 us (94%)
  local copies, waits for them, and re-layouts  2.44 us (4%)
  between operations  0.64 us (1%)
    pallas_call x1, Pallas kernels, per_device(): pl.pallas_call(kernel, out_shape=(jax.ShapeDtypeStruct((tokens, value_up....  54.3 us
    unnamed x2, local copies, waits for them, and re-layouts  2.44 us

profile of v2, /device:TPU:1, one launch (start us, length us, event | category | flops | bytes accessed | tf_op | source)
XLA Modules:
  0.0 57.4 jit_solution(16371519192436246421)
XLA Ops:
  0.6 54.3 %shard_map.113 = (bf16[4,128]{1,0:T(4,128)(2,1)}, bf16[4,56]{1,0:T(4,128)(2,1)}) custom-call(s32[2]{0:T(128)} %lengths.1, bf16[2,576,6144]{2,1,0:T(8,128)(2,1)} %bitcast.4, bf16[2,2,576,128]{3,2,1,0:T(8,128)(2,1)} %bitcast.7, bf16[4,7168]{1,0:T(4,128)(2,1)} %residual.1, bf16[1,512,128]{2,1,0:T(8,128)(2,1)} %value_up.1, bf16[128,7168]{1,0:T(8,128)(2,1)} %out_w.1, ...), custom_call_target="tpu_custom_call" | custom-call | tf_op jit(solution)/shard_map/pallas_call | solution.py:394
  54.9 1.2 %copy.14 = bf16[4,128]{1,0:T(4,128)(2,1)} copy(bf16[4,128]{1,0:T(4,128)(2,1)} %get-tuple-element.4) | data formatting | bytes 2048
  56.2 1.2 %copy.15 = bf16[4,56]{1,0:T(4,128)(2,1)} copy(bf16[4,56]{1,0:T(4,128)(2,1)} %get-tuple-element.5) | data formatting | bytes 896

commit v3 on v2

--- a/solution.py
+++ b/solution.py
@@ -12,6 +12,7 @@
 SCALE = (NOPE + ROPE) ** (-0.5)
 NEG = -1e30
 CHUNK = 1024
+AHEAD = 2
 BF = jnp.bfloat16
 F32 = jnp.float32
 NT = (((1,), (1,)), ((), ()))
@@ -114,11 +115,13 @@
     for r in range(requests):
         for c in range(chunks):
             part = pl.ds(c * CHUNK, CHUNK)
-            copy = pltpu.make_async_copy(
-                cache.at[r, :, part], kbuf.at[r, :, part], ksem.at[r * chunks + c]
+            kcopies.append(
+                pltpu.make_async_copy(
+                    cache.at[r, :, part], kbuf.at[r, :, part], ksem.at[r * chunks + c]
+                )
             )
-            copy.start()
-            kcopies.append(copy)
+    for copy in kcopies[:AHEAD]:
+        copy.start()
     weights = [
         pltpu.make_async_copy(src, dst, wsem.at[i + 1])
         for i, (src, dst) in enumerate(
@@ -172,6 +175,8 @@
         for c in range(chunks):
             part = pl.ds(c * CHUNK, CHUNK)
             kcopies[r * chunks + c].wait()
+            if r == 0:
+                kcopies[c + AHEAD].start()
             s = jnp.dot(q, kbuf[r, :, part], preferred_element_type=F32)
             pos = first + c * CHUNK + lax.broadcasted_iota(jnp.int32, (1, CHUNK), 1)
             halves = []
@@ -191,6 +196,8 @@
         numer = jnp.zeros((qrows, latent), F32)
         for c in range(chunks):
             part = pl.ds(c * CHUNK, CHUNK)
+            if r == 0 and c < chunks - AHEAD:
+                kcopies[chunks + AHEAD + c].start()
             w = jnp.exp2(sbuf[:, part] * factor - shift)
             for t in range(CHUNK // 128):
                 total = total + w[:, t * 128 : (t + 1) * 128]
@@ -259,11 +266,10 @@
     for c in range((pieces + 3) * nq, x2.shape[1]):
         x2[:, c, :] = jnp.zeros((chips, 128), F32)
     qcopy.wait()
-    top = scores(0)
+    values(0, scores(0))
+    top = scores(1)
     for copy in weights:
         copy.start()
-    values(0, top)
-    top = scores(1)
     exchange(0)
     values(1, top)
     exchange(1)
@@ -333,6 +339,17 @@
         sent(5 + step, rcv4.at[step])
     sent(8, rcv5)
     sent(9, rcv6)
+
+
+def hand_on(head_values, mixed, head_values_out, mixed_out, sems):
+    copies = [
+        pltpu.make_async_copy(head_values, head_values_out, sems.at[0]),
+        pltpu.make_async_copy(mixed, mixed_out, sems.at[1]),
+    ]
+    for copy in copies:
+        copy.start()
+    for copy in copies:
+        copy.wait()
 
 
 def per_device(
@@ -391,7 +408,7 @@
         pltpu.SemaphoreType.DMA((10,)),
     ]
     anywhere = pl.BlockSpec(memory_space=pl.ANY)
-    return pl.pallas_call(
+    results = pl.pallas_call(
         kernel,
         out_shape=(
             jax.ShapeDtypeStruct((tokens, value_up.shape[0] * value_up.shape[2]), BF),
@@ -415,6 +432,13 @@
         up_weight,
         down_weight,
     )
+    return pl.pallas_call(
+        hand_on,
+        out_shape=tuple(jax.ShapeDtypeStruct(x.shape, x.dtype) for x in results),
+        in_specs=[anywhere] * 2,
+        out_specs=(anywhere,) * 2,
+        scratch_shapes=[pltpu.SemaphoreType.DMA((2,))],
+    )(*results)
 
 
 def solution(mesh):

time: 57.5 us -> 53.3 us (0.927)
  local copies, waits for them, and re-layouts: 2.44 us -> 0 us
  Pallas kernels: 54.3 us -> 52.4 us
    pallas_call x1, Pallas kernels: 54.3 us -> 51.3 us  [per_device(): pl.pallas_call(kernel, out_shape=(jax.ShapeDtypeStruct((tokens, value_up....]
    unnamed x2 -> x0, local copies, waits for them, and re-layouts: 2.44 us -> none
    pallas_call x0 -> x1, Pallas kernels: none -> 1.18 us  [per_device(): pl.pallas_call(hand_on, out_shape=tuple((jax.ShapeDtypeStruct(x.shape, x....]
where the time goes in v3:
time: 53.3 us; the launch traced here: 53.1 us
  Pallas kernels  52.4 us (98%)
  between operations  0.64 us (1%)
    pallas_call x1, Pallas kernels, per_device(): pl.pallas_call(kernel, out_shape=(jax.ShapeDtypeStruct((tokens, value_up....  51.3 us
    pallas_call x1, Pallas kernels, per_device(): pl.pallas_call(hand_on, out_shape=tuple((jax.ShapeDtypeStruct(x.shape, x....  1.18 us

profile of v3, /device:TPU:1, one launch (start us, length us, event | category | flops | bytes accessed | tf_op | source)
XLA Modules:
  0.0 53.1 jit_solution(10785226623650751714)
XLA Ops:
  0.6 51.3 %shard_map.113 = (bf16[4,128]{1,0:T(4,128)(2,1)}, bf16[4,56]{1,0:T(4,128)(2,1)}) custom-call(s32[2]{0:T(128)} %lengths.1, bf16[2,576,6144]{2,1,0:T(8,128)(2,1)} %bitcast.4, bf16[2,2,576,128]{3,2,1,0:T(8,128)(2,1)} %bitcast.7, bf16[4,7168]{1,0:T(4,128)(2,1)} %residual.1, bf16[1,512,128]{2,1,0:T(8,128)(2,1)} %value_up.1, bf16[128,7168]{1,0:T(8,128)(2,1)} %out_w.1, ...), custom_call_target="tpu_custom_call" | custom-call | tf_op jit(solution)/shard_map/pallas_call | solution.py:411
  51.9 1.2 %shard_map.114 = (bf16[4,128]{1,0:T(4,128)(2,1)}, bf16[4,56]{1,0:T(4,128)(2,1)}) custom-call(bf16[4,128]{1,0:T(4,128)(2,1)} %get-tuple-element.4.head_values, bf16[4,56]{1,0:T(4,128)(2,1)} %get-tuple-element.5.mixed), custom_call_target="tpu_custom_call" | custom-call | tf_op jit(solution)/shard_map/pallas_call | solution.py:435

commit v4 on v3

--- a/solution.py
+++ b/solution.py
@@ -12,6 +12,7 @@
 SCALE = (NOPE + ROPE) ** (-0.5)
 NEG = -1e30
 CHUNK = 1024
+WIDE = 3072
 AHEAD = 2
 BF = jnp.bfloat16
 F32 = jnp.float32
@@ -172,20 +173,23 @@
             axis=0,
         )
         peak = None
-        for c in range(chunks):
-            part = pl.ds(c * CHUNK, CHUNK)
-            kcopies[r * chunks + c].wait()
+        span = CHUNK if r == 0 else WIDE
+        for c in range(rows // span):
+            part = pl.ds(c * span, span)
+            at = r * chunks + c * span // CHUNK
+            for copy in kcopies[at : at + span // CHUNK]:
+                copy.wait()
             if r == 0:
                 kcopies[c + AHEAD].start()
             s = jnp.dot(q, kbuf[r, :, part], preferred_element_type=F32)
-            pos = first + c * CHUNK + lax.broadcasted_iota(jnp.int32, (1, CHUNK), 1)
+            pos = first + c * span + lax.broadcasted_iota(jnp.int32, (1, span), 1)
             halves = []
             for j in range(nq):
                 bias = jnp.where(pos < lengths[r] - (nq - 1) + j, 0.0, NEG)
                 halves.append(s[j * heads : (j + 1) * heads] + bias)
             s = jnp.concatenate(halves, axis=0)
             sbuf[:, part] = s
-            for t in range(CHUNK // 128):
+            for t in range(span // 128):
                 tile = s[:, t * 128 : (t + 1) * 128]
                 peak = tile if peak is None else jnp.maximum(peak, tile)
         return jnp.max(peak, axis=1, keepdims=True)
@@ -194,12 +198,13 @@
         shift = top * factor
         total = jnp.zeros((qrows, 128), F32)
         numer = jnp.zeros((qrows, latent), F32)
-        for c in range(chunks):
-            part = pl.ds(c * CHUNK, CHUNK)
+        span = CHUNK if r == 0 else WIDE
+        for c in range(rows // span):
+            part = pl.ds(c * span, span)
             if r == 0 and c < chunks - AHEAD:
                 kcopies[chunks + AHEAD + c].start()
             w = jnp.exp2(sbuf[:, part] * factor - shift)
-            for t in range(CHUNK // 128):
+            for t in range(span // 128):
                 total = total + w[:, t * 128 : (t + 1) * 128]
             numer = numer + lax.dot_general(
                 w.astype(BF), kbuf[r, :latent, part], NT, preferred_element_type=F32

time: 53.3 us -> 52.6 us (0.987)
  Pallas kernels: 52.4 us -> 51.7 us
    pallas_call x1, Pallas kernels: 51.3 us -> 50.6 us  [per_device(): pl.pallas_call(kernel, out_shape=(jax.ShapeDtypeStruct((tokens, value_up....]
where the time goes in v4:
time: 52.6 us; the launch traced here: 52.4 us
  Pallas kernels  51.7 us (98%)
  between operations  0.64 us (1%)
    pallas_call x1, Pallas kernels, per_device(): pl.pallas_call(kernel, out_shape=(jax.ShapeDtypeStruct((tokens, value_up....  50.6 us
    pallas_call x1, Pallas kernels, per_device(): pl.pallas_call(hand_on, out_shape=tuple((jax.ShapeDtypeStruct(x.shape, x....  1.18 us

profile of v4, /device:TPU:1, one launch (start us, length us, event | category | flops | bytes accessed | tf_op | source)
XLA Modules:
  0.0 52.4 jit_solution(16183494691706286461)
XLA Ops:
  0.6 50.6 %shard_map.113 = (bf16[4,128]{1,0:T(4,128)(2,1)}, bf16[4,56]{1,0:T(4,128)(2,1)}) custom-call(s32[2]{0:T(128)} %lengths.1, bf16[2,576,6144]{2,1,0:T(8,128)(2,1)} %bitcast.4, bf16[2,2,576,128]{3,2,1,0:T(8,128)(2,1)} %bitcast.7, bf16[4,7168]{1,0:T(4,128)(2,1)} %residual.1, bf16[1,512,128]{2,1,0:T(8,128)(2,1)} %value_up.1, bf16[128,7168]{1,0:T(8,128)(2,1)} %out_w.1, ...), custom_call_target="tpu_custom_call" | custom-call | tf_op jit(solution)/shard_map/pallas_call | solution.py:416
  51.2 1.2 %shard_map.114 = (bf16[4,128]{1,0:T(4,128)(2,1)}, bf16[4,56]{1,0:T(4,128)(2,1)}) custom-call(bf16[4,128]{1,0:T(4,128)(2,1)} %get-tuple-element.4.head_values, bf16[4,56]{1,0:T(4,128)(2,1)} %get-tuple-element.5.mixed), custom_call_target="tpu_custom_call" | custom-call | tf_op jit(solution)/shard_map/pallas_call | solution.py:440

commit v5 on v4

--- a/solution.py
+++ b/solution.py
@@ -161,17 +161,16 @@
     first = (a * 16 + b) * rows
     factor = SCALE * math.log2(math.e)
 
-    def scores(r):
-        at = lax.broadcasted_iota(jnp.int32, (heads, heads), 0)
-        head = lax.broadcasted_iota(jnp.int32, (heads, heads), 1)
-        order = jnp.where(head == (at % chips) * 2 + at // chips, 1.0, 0.0).astype(BF)
-        q = jnp.concatenate(
+    def ordered(r, order):
+        return jnp.concatenate(
             [
                 lax.dot_general(order, qbuf[r, j], NT, preferred_element_type=F32).astype(BF)
                 for j in range(nq)
             ],
             axis=0,
         )
+
+    def scores(r, q):
         peak = None
         span = CHUNK if r == 0 else WIDE
         for c in range(rows // span):
@@ -270,9 +269,13 @@
 
     for c in range((pieces + 3) * nq, x2.shape[1]):
         x2[:, c, :] = jnp.zeros((chips, 128), F32)
+    at = lax.broadcasted_iota(jnp.int32, (heads, heads), 0)
+    head = lax.broadcasted_iota(jnp.int32, (heads, heads), 1)
+    order = jnp.where(head == (at % chips) * 2 + at // chips, 1.0, 0.0).astype(BF)
     qcopy.wait()
-    values(0, scores(0))
-    top = scores(1)
+    qs = [ordered(r, order) for r in range(requests)]
+    values(0, scores(0, qs[0]))
+    top = scores(1, qs[1])
     for copy in weights:
         copy.start()
     exchange(0)

time: 52.6 us -> 52.5 us (level)
  no operation moved by 1% of the time
where the time goes in v5:
time: 52.5 us; the launch traced here: 52.2 us
  Pallas kernels  51.6 us (98%)
  between operations  0.64 us (1%)
    pallas_call x1, Pallas kernels, per_device(): pl.pallas_call(kernel, out_shape=(jax.ShapeDtypeStruct((tokens, value_up....  50.4 us
    pallas_call x1, Pallas kernels, per_device(): pl.pallas_call(hand_on, out_shape=tuple((jax.ShapeDtypeStruct(x.shape, x....  1.18 us

profile of v5, /device:TPU:1, one launch (start us, length us, event | category | flops | bytes accessed | tf_op | source)
XLA Modules:
  0.0 52.2 jit_solution(16908202595752171197)
XLA Ops:
  0.6 50.4 %shard_map.113 = (bf16[4,128]{1,0:T(4,128)(2,1)}, bf16[4,56]{1,0:T(4,128)(2,1)}) custom-call(s32[2]{0:T(128)} %lengths.1, bf16[2,576,6144]{2,1,0:T(8,128)(2,1)} %bitcast.4, bf16[2,2,576,128]{3,2,1,0:T(8,128)(2,1)} %bitcast.7, bf16[4,7168]{1,0:T(4,128)(2,1)} %residual.1, bf16[1,512,128]{2,1,0:T(8,128)(2,1)} %value_up.1, bf16[128,7168]{1,0:T(8,128)(2,1)} %out_w.1, ...), custom_call_target="tpu_custom_call" | custom-call | tf_op jit(solution)/shard_map/pallas_call | solution.py:419
  51.1 1.2 %shard_map.114 = (bf16[4,128]{1,0:T(4,128)(2,1)}, bf16[4,56]{1,0:T(4,128)(2,1)}) custom-call(bf16[4,128]{1,0:T(4,128)(2,1)} %get-tuple-element.4.head_values, bf16[4,56]{1,0:T(4,128)(2,1)} %get-tuple-element.5.mixed), custom_call_target="tpu_custom_call" | custom-call | tf_op jit(solution)/shard_map/pallas_call | solution.py:443
